TPU v7x, 32 devices: a whole 2x2x4 slice. The times are simulated.
32 devices in a mesh: clip: 8 (over z, x), freq: 4 (over y, core).
Axes of the slice: x: 2, y: 2, z: 4, core: 2. Of those that a mesh axis runs over, the one named last changes fastest.
Arguments:
- tokens: bfloat16 [8, 1188, 768], P('clip', 'freq'), may hold values from -6 to 6
- grad_out: bfloat16 [8, 1188, 768], P('clip', 'freq'), may hold values from -6 to 6
- freq_keep: int32 [8, 12], P('clip'), may hold values from 0 to 1, as said below
- lengths: int32 [8], P('clip'), may hold values from 49 to 99
- first_gain: float32 [768], replicated, may hold values from 0.25 to 1.75
- first_shift: float32 [768], replicated, may hold values from -1.75 to 1.75
- qkv_weight: bfloat16 [768, 2304], replicated, may hold values from -0.21875 to 0.21875
- query_bias: float32 [768], replicated, may hold values from -1.75 to 1.75
- value_bias: float32 [768], replicated, may hold values from -0.1875 to 0.1875
- proj_weight: bfloat16 [768, 768], replicated, may hold values from -4 to 4
- proj_bias: float32 [768], replicated, may hold values from -1.75 to 1.75
- second_gain: float32 [768], replicated, may hold values from 0.25 to 1.75
- second_shift: float32 [768], replicated, may hold values from -1.75 to 1.75
- up_weight: bfloat16 [768, 3072], replicated, may hold values from -0.21875 to 0.21875
- up_bias: float32 [3072], replicated, may hold values from -1.75 to 1.75
- down_weight: bfloat16 [3072, 768], replicated, may hold values from -0.109375 to 0.109375
- down_bias: float32 [768], replicated, may hold values from -1.75 to 1.75
Outputs:
- block_out: bfloat16 [8, 1188, 768], P('clip', 'freq')
- grad_tokens: bfloat16 [8, 1188, 768], P('clip', 'freq')
- grad_first_gain: float32 [768], P(('clip', 'freq'))
- grad_first_shift: float32 [768], P(('clip', 'freq'))
- grad_qkv_weight: float32 [768, 2304], P(('clip', 'freq'))
- grad_query_bias: float32 [768], P(('clip', 'freq'))
- grad_value_bias: float32 [768], P(('clip', 'freq'))
- grad_proj_weight: float32 [768, 768], P(('clip', 'freq'))
- grad_proj_bias: float32 [768], P(('clip', 'freq'))
- grad_second_gain: float32 [768], P(('clip', 'freq'))
- grad_second_shift: float32 [768], P(('clip', 'freq'))
- grad_up_weight: float32 [768, 3072], P(('clip', 'freq'))
- grad_up_bias: float32 [3072], P(('clip', 'freq'))
- grad_down_weight: float32 [3072, 768], P(('clip', 'freq'))
- grad_down_bias: float32 [768], P(('clip', 'freq'))
Inputs may be any that keep to these rules, and one draw needn't show every extreme that they name: `freq_keep`: every clip keeps at least one frequency row among those of each index of freq.
All inputs are finite; a program needn't handle non-finite values.
Results may differ from a plain program's by a relative error of at most 0.014.
Values may be sent and summed in bfloat16 or wider, within the bound.
A program may use at most 128 MiB of HBM per device.

v0:
```python
import jax
import jax.numpy as jnp
from jax import lax
from jax.sharding import PartitionSpec as P

HEADS = 12
TIME_COLS = 99


EPS = 1e-06


def layer_stats(values):
    center = values - jnp.mean(values, -1, keepdims=True)
    inv_std = lax.rsqrt(jnp.mean(center * center, -1, keepdims=True) + EPS)
    return (center * inv_std, inv_std)


def norm_back(grad_norm, normed, inv_std, gain):
    scaled = grad_norm * gain
    return inv_std * (
        scaled
        - jnp.mean(scaled, -1, keepdims=True)
        - normed * jnp.mean(scaled * normed, -1, keepdims=True)
    )


def outer_sum(left, right):
    return jnp.einsum("crd,cre->de", left, right, preferred_element_type=jnp.float32)


def column_sum(grad_rows):
    return jnp.sum(grad_rows.astype(jnp.float32), axis=(0, 1))


def back_dot(grad_rows, weight):
    return lax.dot_general(
        grad_rows, weight, (((2,), (1,)), ((), ())), preferred_element_type=jnp.float32
    )


def on_device(
    tokens,
    grad_out,
    freq_keep,
    lengths,
    first_gain,
    first_shift,
    qkv_weight,
    query_bias,
    value_bias,
    proj_weight,
    proj_bias,
    second_gain,
    second_shift,
    up_weight,
    up_bias,
    down_weight,
    down_bias,
):
    clip_count, row_count, model_width = tokens.shape
    head_count = HEADS
    head_size = model_width // head_count
    slot_count = row_count * lax.axis_size("freq")
    columns = jnp.arange(TIME_COLS, dtype=jnp.int32)
    live = (freq_keep[:, :, None] > 0) & (columns[None, None, :] < lengths[:, None, None])
    key_mask = live.reshape(clip_count, slot_count)
    row_start = lax.axis_index("freq") * row_count
    keep = lax.dynamic_slice_in_dim(key_mask, row_start, row_count, 1).astype(jnp.float32)[
        :, :, None
    ]
    inputs = tokens.astype(jnp.float32)
    normed_one, inv_one = layer_stats(inputs)
    first_in = (normed_one * first_gain + first_shift).astype(jnp.bfloat16)
    projected = jnp.dot(first_in, qkv_weight, preferred_element_type=jnp.float32)
    queries = (projected[..., :model_width] + query_bias).astype(jnp.bfloat16)
    key_rows = projected[..., model_width : 2 * model_width].astype(jnp.bfloat16)
    value_rows = (projected[..., 2 * model_width :] + value_bias).astype(jnp.bfloat16)
    key_all, value_all = (
        lax.all_gather(key_rows, "freq", axis=1, tiled=True),
        lax.all_gather(value_rows, "freq", axis=1, tiled=True),
    )

    def head_split(rows_in):
        return rows_in.reshape(rows_in.shape[0], rows_in.shape[1], head_count, head_size)

    q_heads = head_split(queries)

    def scores_of(key_whole):
        raw = (
            jnp.einsum(
                "crhd,cshd->chrs",
                q_heads,
                head_split(key_whole),
                preferred_element_type=jnp.float32,
            )
            * 0.125
        )
        return jnp.where(key_mask[:, None, None, :], raw, -1e30)

    scores = scores_of(key_all)
    row_max = jnp.max(scores, -1, keepdims=True)
    exp_scores = jnp.exp(scores - row_max)
    row_total = jnp.sum(exp_scores, -1, keepdims=True)
    attn_prob = exp_scores / row_total
    log_total = row_max + jnp.log(row_total)
    prob_low = attn_prob.astype(jnp.bfloat16)
    mixed_heads = jnp.einsum(
        "chrs,cshd->crhd", prob_low, head_split(value_all), preferred_element_type=jnp.float32
    )
    attn_rows = mixed_heads.reshape(clip_count, row_count, model_width).astype(jnp.bfloat16)
    mid_rows = inputs + (
        jnp.dot(attn_rows, proj_weight, preferred_element_type=jnp.float32) + proj_bias
    )
    normed_two, inv_two = layer_stats(mid_rows)
    second_in = (normed_two * second_gain + second_shift).astype(jnp.bfloat16)
    pre_act = jnp.dot(second_in, up_weight, preferred_element_type=jnp.float32) + up_bias
    hidden_rows = jax.nn.gelu(pre_act, approximate=False).astype(jnp.bfloat16)
    ff_out = jnp.dot(hidden_rows, down_weight, preferred_element_type=jnp.float32) + down_bias
    block_out = (keep * (mid_rows + ff_out)).astype(jnp.bfloat16)
    grad_kept = keep * grad_out.astype(jnp.float32)
    grad_low = grad_kept.astype(jnp.bfloat16)
    g_down_weight = outer_sum(hidden_rows, grad_low)
    g_down_bias = column_sum(grad_low)
    d_hidden = back_dot(grad_low, down_weight)
    unused_out, gelu_pull = jax.vjp(lambda inner: jax.nn.gelu(inner, approximate=False), pre_act)
    d_pre = gelu_pull(d_hidden)[0].astype(jnp.bfloat16)
    g_up_weight = outer_sum(second_in, d_pre)
    g_up_bias = column_sum(d_pre)
    d_second = back_dot(d_pre, up_weight)
    g_second_gain = jnp.sum(d_second * normed_two, axis=(0, 1))
    g_second_shift = jnp.sum(d_second, axis=(0, 1))
    d_mid = grad_kept + norm_back(d_second, normed_two, inv_two, second_gain)
    d_branch = d_mid.astype(jnp.bfloat16)
    g_proj_weight = outer_sum(attn_rows, d_branch)
    g_proj_bias = column_sum(d_branch)
    d_attn = back_dot(d_branch, proj_weight).astype(jnp.bfloat16)
    key_back, value_back = (key_all, value_all)
    prob_back = jnp.exp(scores_of(key_back) - log_total)
    d_heads = head_split(d_attn)
    d_prob = jnp.einsum(
        "crhd,cshd->chrs", d_heads, head_split(value_back), preferred_element_type=jnp.float32
    )
    d_score = (prob_back * (d_prob - jnp.sum(prob_back * d_prob, -1, keepdims=True))).astype(
        jnp.bfloat16
    )
    d_queries = (
        jnp.einsum(
            "chrs,cshd->crhd", d_score, head_split(key_back), preferred_element_type=jnp.float32
        )
        * 0.125
    )
    d_queries = d_queries.reshape(clip_count, row_count, model_width).astype(jnp.bfloat16)
    d_key_all = (
        jnp.einsum("chrs,crhd->cshd", d_score, q_heads, preferred_element_type=jnp.float32) * 0.125
    )
    d_key_all = d_key_all.reshape(clip_count, slot_count, model_width)
    d_value_all = jnp.einsum(
        "chrs,crhd->cshd",
        prob_back.astype(jnp.bfloat16),
        d_heads,
        preferred_element_type=jnp.float32,
    )
    d_value_all = d_value_all.reshape(clip_count, slot_count, model_width)
    d_key_sum, d_value_sum = (
        lax.psum_scatter(
            d_key_all.astype(jnp.bfloat16), "freq", scatter_dimension=1, tiled=True
        ).astype(jnp.float32),
        lax.psum_scatter(
            d_value_all.astype(jnp.bfloat16), "freq", scatter_dimension=1, tiled=True
        ).astype(jnp.float32),
    )
    d_keys = d_key_sum.astype(jnp.bfloat16)
    d_values = d_value_sum.astype(jnp.bfloat16)
    d_qkv = jnp.concatenate([d_queries, d_keys, d_values], axis=-1)
    g_qkv_weight = outer_sum(first_in, d_qkv)
    g_query_bias = column_sum(d_queries)
    g_value_bias = column_sum(d_values)
    d_first = back_dot(d_qkv, qkv_weight)
    g_first_gain = jnp.sum(d_first * normed_one, axis=(0, 1))
    g_first_shift = jnp.sum(d_first, axis=(0, 1))
    grad_tokens = (d_mid + norm_back(d_first, normed_one, inv_one, first_gain)).astype(jnp.bfloat16)
    every_sum = (
        lax.psum_scatter(g_first_gain, ("clip", "freq"), scatter_dimension=0, tiled=True),
        lax.psum_scatter(g_first_shift, ("clip", "freq"), scatter_dimension=0, tiled=True),
        lax.psum_scatter(g_qkv_weight, ("clip", "freq"), scatter_dimension=0, tiled=True),
        lax.psum_scatter(g_query_bias, ("clip", "freq"), scatter_dimension=0, tiled=True),
        lax.psum_scatter(g_value_bias, ("clip", "freq"), scatter_dimension=0, tiled=True),
        lax.psum_scatter(g_proj_weight, ("clip", "freq"), scatter_dimension=0, tiled=True),
        lax.psum_scatter(g_proj_bias, ("clip", "freq"), scatter_dimension=0, tiled=True),
        lax.psum_scatter(g_up_weight, ("clip", "freq"), scatter_dimension=0, tiled=True),
        lax.psum_scatter(g_up_bias, ("clip", "freq"), scatter_dimension=0, tiled=True),
        lax.psum_scatter(g_down_weight, ("clip", "freq"), scatter_dimension=0, tiled=True),
        lax.psum_scatter(g_down_bias, ("clip", "freq"), scatter_dimension=0, tiled=True),
        lax.psum_scatter(g_second_gain, ("clip", "freq"), scatter_dimension=0, tiled=True),
        lax.psum_scatter(g_second_shift, ("clip", "freq"), scatter_dimension=0, tiled=True),
    )
    (
        sum_first_gain,
        sum_first_shift,
        sum_qkv_weight,
        sum_query_bias,
        sum_value_bias,
        sum_proj_weight,
        sum_proj_bias,
        sum_up_weight,
        sum_up_bias,
        sum_down_weight,
        sum_down_bias,
        sum_second_gain,
        sum_second_shift,
    ) = every_sum
    return (
        block_out,
        grad_tokens,
        sum_first_gain,
        sum_first_shift,
        sum_qkv_weight,
        sum_query_bias,
        sum_value_bias,
        sum_proj_weight,
        sum_proj_bias,
        sum_second_gain,
        sum_second_shift,
        sum_up_weight,
        sum_up_bias,
        sum_down_weight,
        sum_down_bias,
    )


def solution(mesh):
    placed = (
        P("clip", "freq", None),
        P("clip", "freq", None),
        P("clip", None),
        P("clip"),
        P(),
        P(),
        P(),
        P(),
        P(),
        P(),
        P(),
        P(),
        P(),
        P(),
        P(),
        P(),
        P(),
    )
    return jax.shard_map(
        on_device,
        mesh=mesh,
        in_specs=placed,
        out_specs=(
            P("clip", "freq", None),
            P("clip", "freq", None),
            P(("clip", "freq")),
            P(("clip", "freq")),
            P(("clip", "freq"), None),
            P(("clip", "freq")),
            P(("clip", "freq")),
            P(("clip", "freq"), None),
            P(("clip", "freq")),
            P(("clip", "freq")),
            P(("clip", "freq")),
            P(("clip", "freq"), None),
            P(("clip", "freq")),
            P(("clip", "freq"), None),
            P(("clip", "freq")),
        ),
        check_vma=False,
    )
```

profile of v0, /device:TPU:0, one launch (start us, length us, event | category | flops | bytes accessed | tf_op | source)
XLA Modules:
  0.0 770.5 jit_solution(18077938810072031588)
XLA Ops:
  7.2 1.3 convert_reduce_fusion.1
  8.6 1.3 fusion.38
  10.5 2.4 convolution_bitcast_fusion
  12.9 1.5 copy-done.15
  14.5 1.7 copy.47
  16.3 2.4 fusion.39
  18.7 1.6 copy.44
  21.9 0.7 and.43
  22.6 0.7 and.40
  23.2 2.1 copy.46
  25.3 0.7 and.44
  26.0 0.8 fusion.60
  26.8 23.7 %all-gather.5.cloned.1.call-done = bf16[1,1188,768]{2,0,1:T(2,128)(2,1)} async-done(((bf16[1,297,768]{2,0,1:T(2,128)(2,1)}), bf16[1,1188,768]{2,0,1:T(2,128)(2,1)}) %all-gather.5.cloned.1.call-update) | async-done | bytes 1824784 | tf_op jit(solution)/shard_map/all_gather | solution.py:80
  50.5 8.6 %copy.48 = bf16[1,1188,768]{1,2,0:T(8,128)(2,1)} copy(bf16[1,1188,768]{2,0,1:T(2,128)(2,1)} %all-gather.5.cloned.1.call-done) | data formatting | bytes 3649536 | tf_op jit(solution)/shard_map/all_gather | solution.py:80
  59.0 11.8 %fusion.76 = (f32[12,297]{1,0:T(8,128)}, f32[12,297,1188]{2,1,0:T(8,128)}) fusion(bf16[297,12,64]{0,2,1:T(8,128)(2,1)} %bitcast.136, bf16[1188,12,64]{0,2,1:T(8,128)(2,1)} %bitcast.130, pred[1188]{0:T(1024)(128)(4,1)S(1)} %and.44), kind=kOutput, calls=%fused_computation.122 | convolution fusion | flops 554654656 | bytes 19232532 | tf_op jit(solution)/shard_map/crhd,cshd->chrs/dot_general | solution.py:91
  70.8 9.8 %fusion.1 = f32[12,297]{1,0:T(8,128)} fusion(f32[12,297,1188]{2,1,0:T(8,128)} %get-tuple-element.44, f32[12,297]{1,0:T(8,128)} %get-tuple-element.43), kind=kLoop, calls=%fused_computation.7 | loop fusion | flops 8464500 | bytes 16964640 | tf_op jit(solution)/shard_map/reduce_sum | solution.py:104
  80.6 1.4 log_add_fusion
  81.9 1.5 all-gather.3.cloned.1.call-done
  83.5 8.6 %copy.45 = bf16[1,1188,768]{1,2,0:T(8,128)(2,1)} copy(bf16[1,1188,768]{2,0,1:T(2,128)(2,1)} %all-gather.3.cloned.1.call-done) | data formatting | bytes 3649536 | tf_op jit(solution)/shard_map/all_gather | solution.py:81
  92.0 8.9 %fusion.18 = bf16[12,64,297]{2,1,0:T(8,128)(2,1)S(1)} fusion(bf16[1188,12,64]{0,2,1:T(8,128)(2,1)} %bitcast.134, f32[12,297,1188]{2,1,0:T(8,128)} %get-tuple-element.44, f32[12,297]{1,0:T(8,128)} %fusion.1, f32[12,297]{1,0:T(8,128)} %get-tuple-element.43), kind=kOutput, calls=%fused_computation.42 | convolution fusion | flops 554886272 | bytes 19245600 | tf_op jit(solution)/shard_map/chrs,cshd->crhd/dot_general | solution.py:108
  101.0 0.7 fusion.77
  102.1 13.1 %multiply_convert_fusion.1 = (bf16[297,3072]{1,0:T(8,128)(2,1)}, f32[297,3072]{1,0:T(8,128)S(1)}, f32[297,3072]{1,0:T(8,128)S(1)}) fusion(f32[3072]{0:T(1024)S(1)} %copy-done.35, bf16[768,3072]{1,0:T(8,128)(2,1)} %param.30, f32[1,297,768]{2,1,0:T(8,128)S(1)} %get-tuple-element.46, f32[768]{0:T(1024)S(1)} %copy-done.22, f32[768]{0:T(1024)S(1)} %copy-done.21, ...), kind=kOutput, calls=%fused_computation.19 | convolution fusion | flops 1462779648 | bytes 14775624 | tf_op jit(solution)/shard_map/dot_general | solution.py:117
  115.2 4.3 convert_reduce_fusion
  119.4 2.3 fusion.41
  121.8 0.7 fusion.72
  122.5 1.1 convert_reduce_fusion.5
  123.6 0.9 copy-done.2
  124.5 1.3 convolution_convert_fusion
  125.8 2.1 copy.49
  127.9 11.0 %fusion.14 = bf16[12,64,1188]{2,1,0:T(8,128)(2,1)} fusion(bf16[297,12,64]{0,2,1:T(8,128)(2,1)} %bitcast.138, f32[12,297,1188]{2,1,0:T(8,128)} %get-tuple-element.44, f32[12,297]{1,0:T(8,128)} %log_add_fusion), kind=kOutput, calls=%fused_computation.34 | convolution fusion | flops 551336576 | bytes 19231344 | tf_op jit(solution)/shard_map/chrs,crhd->cshd/dot_general | solution.py:158
  138.9 12.4 %multiply_reduce_fusion = (f32[12,297]{1,0:T(8,128)S(1)}, f32[12,297,1188]{2,1,0:T(8,128)}) fusion(f32[12,297,1188]{2,1,0:T(8,128)} %get-tuple-element.44, f32[12,297]{1,0:T(8,128)S(1)} %copy-done.20, bf16[297,12,64]{0,2,1:T(8,128)(2,1)S(1)} %bitcast.139, bf16[1188,12,64]{0,2,1:T(8,128)(2,1)S(1)} %bitcast.135), kind=kOutput, calls=%fused_computation.3 | convolution fusion | flops 554654656 | bytes 36181728 | tf_op jit(solution)/shard_map/crhd,cshd->chrs/dot_general | solution.py:141
  151.4 12.8 %multiply_convert_fusion = bf16[12,297,1188]{2,1,0:T(8,128)(2,1)S(1)} fusion(f32[12,297,1188]{2,1,0:T(8,128)} %get-tuple-element.50, f32[12,297,1188]{2,1,0:T(8,128)} %get-tuple-element.44, f32[12,297]{1,0:T(8,128)S(1)} %get-tuple-element.49, f32[12,297]{1,0:T(8,128)S(1)} %copy-done.20), kind=kLoop, calls=%fused_computation.2 | loop fusion | flops 16936128 | bytes 42368832 | tf_op jit(solution)/shard_map/convert_element_type | solution.py:144
  164.2 3.9 fusion.13
  168.6 3.5 fusion.50
  173.4 8.8 %convert_reduce_fusion.3 = (f32[12,64]{1,0:T(8,128)}, bf16[12,64,297]{2,1,0:T(8,128)(2,1)}) fusion(bf16[1188,12,64]{0,2,1:T(8,128)(2,1)} %bitcast.131, bf16[12,297,1188]{2,1,0:T(8,128)(2,1)} %copy-done.1), kind=kOutput, calls=%fused_computation.51 | convolution fusion | flops 542867712 | bytes 10752096 | tf_op jit(solution)/shard_map/chrs,cshd->crhd/dot_general | solution.py:148
  182.3 67.8 %all-reduce.15.cloned.1.call-done = (bf16[1,1188,768]{1,2,0:T(8,128)(2,1)}, bf16[1,1188,768]{1,2,0:T(8,128)(2,1)}) async-done(((bf16[1,1188,768]{1,2,0:T(8,128)(2,1)}, bf16[1,1188,768]{1,2,0:T(8,128)(2,1)}), (bf16[1,1188,768]{1,2,0:T(8,128)(2,1)}, bf16[1,1188,768]{1,2,0:T(8,128)(2,1)})) %all-reduce.15.cloned.1.call-update) | async-done | bytes 3649552
  250.1 2.2 convert_reduce_fusion.2
  252.3 1.6 constant_dynamic-slice_fusion.1
  253.9 0.8 copy-done.13
  254.7 6.4 fusion.46
  261.4 8.3 %fusion.69 = f32[768,3072]{1,0:T(8,128)} fusion(bf16[297,3072]{1,0:T(8,128)(2,1)} %copy-done.16, f32[1,297,768]{2,1,0:T(8,128)} %copy-done.3, f32[768]{0:T(1024)S(1)} %copy-done.22, f32[768]{0:T(1024)S(1)} %copy-done.21, f32[297]{0:T(512)} %copy-done.25, f32[297]{0:T(512)S(1)} %broadcast_multiply_fusion.4), kind=kOutput, calls=%fused_computation.119 | convolution fusion | flops 1402562304 | bytes 12182856 | tf_op jit(solution)/shard_map/crd,cre->de/dot_general | solution.py:29
  270.4 8.0 %fusion.53 = f32[3072,768]{1,0:T(8,128)} fusion(bf16[297,3072]{1,0:T(8,128)(2,1)} %get-tuple-element.38, bf16[1,297,768]{2,1,0:T(8,128)(2,1)} %param.18, f32[297]{0:T(512)S(1)} %copy-done.29), kind=kOutput, calls=%fused_computation.95 | convolution fusion | flops 1402106112 | bytes 11719332 | tf_op jit(solution)/shard_map/crd,cre->de/dot_general | solution.py:29
  278.4 0.7 copy-done.24
  279.7 5.8 fusion.23
  285.6 2.5 fusion.37
  288.1 0.9 copy-done.9
  289.0 0.8 fusion.73
  289.8 41.3 %all-reduce.11 = (f32[768]{0:T(1024)}, f32[768]{0:T(1024)}, f32[768]{0:T(1024)}, f32[768]{0:T(1024)}, f32[768]{0:T(1024)}, /*index=5*/f32[768]{0:T(1024)}, f32[768]{0:T(1024)}, f32[3072]{0:T(1024)}, f32[768]{0:T(1024)}) all-reduce(f32[768]{0:T(1024)} %get-tuple-element.17, ...), channel_id=4, replica_groups=mesh['clip'=8,'freq'=4] {'clip','freq'}, use_global_device_ids=true, to_apply=%region_14.15.clone | all-reduce | flops 9216 | bytes 73728
  331.1 1.3 dynamic-slice.4
  332.4 1.3 dynamic-slice.5
  333.6 1.3 dynamic-slice.6
  334.9 1.3 dynamic-slice.7
  336.1 1.3 dynamic-slice.8
  337.4 1.3 dynamic-slice.9
  338.7 1.3 dynamic-slice.10
  339.9 1.3 dynamic-slice.12
  341.2 1.3 dynamic-slice.11
  342.5 0.7 broadcast_multiply_fusion
  343.1 0.7 broadcast_multiply_fusion.1
  343.8 2.7 fusion.36
  346.5 8.5 %reduce-scatter.9.cloned.1.call-done = f32[24,768]{1,0:T(8,128)} async-done(((f32[768,768]{1,0:T(8,128)}), f32[24,768]{1,0:T(8,128)}) %reduce-scatter.9.cloned.1.call-update) | async-done | bytes 73744 | tf_op jit(solution)/shard_map/reduce_scatter | solution.py:189
  355.1 125.2 %reduce-scatter.7.cloned.1.call-done = f32[24,2304]{1,0:T(8,128)} async-done(((f32[768,2304]{1,0:T(8,128)}), f32[24,2304]{1,0:T(8,128)}) %reduce-scatter.7.cloned.1.call-update) | async-done | bytes 221200 | tf_op jit(solution)/shard_map/reduce_scatter | solution.py:186
  480.3 141.0 %reduce-scatter.11.cloned.1.call-done = f32[24,3072]{1,0:T(8,128)} async-done(((f32[768,3072]{1,0:T(8,128)}), f32[24,3072]{1,0:T(8,128)}) %reduce-scatter.11.cloned.1.call-update) | async-done | bytes 294928 | tf_op jit(solution)/shard_map/reduce_scatter | solution.py:191
  621.3 142.1 %reduce-scatter.13.cloned.1.call-done = f32[96,768]{1,0:T(8,128)} async-done(((f32[3072,768]{1,0:T(8,128)}), f32[96,768]{1,0:T(8,128)}) %reduce-scatter.13.cloned.1.call-update) | async-done | bytes 294928 | tf_op jit(solution)/shard_map/reduce_scatter | solution.py:193
  (112 shorter events, 4.8 us)
Async XLA Ops:
  7.2 3.3 copy-start
  7.2 43.3 %all-gather.5.cloned.1.call-start = ((), (), s32[]{:S(2)}) async-start(), calls=%async_computation.5 | async-start | bytes 4561920 | tf_op jit(solution)/shard_map/all_gather | solution.py:80
  8.6 1.3 copy-start.26
  9.9 0.6 copy-start.30
  10.5 5.8 copy-start.33
  10.5 5.8 copy-start.34
  12.9 1.5 copy-start.15
  14.5 6.4 copy-start.37
  16.2 67.2 %all-gather.3.cloned.1.call-start = ((), (), s32[]{:S(2)}) async-start(), calls=%async_computation.4 | async-start | bytes 4561920 | tf_op jit(solution)/shard_map/all_gather | solution.py:81
  20.3 229.7 %all-reduce.15.cloned.1.call-start = ((), (), s32[]{:S(2)}) async-start(), calls=%async_computation.10 | async-start | bytes 7864320
  26.8 95.7 %copy-start.28 = (f32[297]{0:T(512)}, f32[297]{0:T(512)S(1)}, u32[]{:S(2)}) copy-start(f32[297]{0:T(512)S(1)} %fusion.60) | copy-start | bytes 3568
  92.0 9.0 %copy-start.5 = (bf16[1,297,768]{2,1,0:T(8,128)(2,1)S(1)}, bf16[1,297,768]{2,1,0:T(8,128)(2,1)}, u32[]{:S(2)}) copy-start(bf16[1,297,768]{2,1,0:T(8,128)(2,1)} %param.17) | copy-start | bytes 1368580
  92.0 9.0 %copy-start.18 = (bf16[768,768]{1,0:T(8,128)(2,1)S(1)}, bf16[768,768]{1,0:T(8,128)(2,1)}, u32[]{:S(2)}) copy-start(bf16[768,768]{1,0:T(8,128)(2,1)} %param.26) | copy-start | bytes 3538948
  92.0 9.0 %copy-start.36 = (f32[768]{0:T(1024)S(1)}, f32[768]{0:T(1024)}, u32[]{:S(2)}) copy-start(f32[768]{0:T(1024)} %param.27) | copy-start | bytes 9220
  100.9 14.2 %copy-start.19 = (bf16[12,64,297]{2,1,0:T(8,128)(2,1)}, bf16[12,64,297]{2,1,0:T(8,128)(2,1)S(1)}, u32[]{:S(2)}) copy-start(bf16[12,64,297]{2,1,0:T(8,128)(2,1)S(1)} %fusion.18) | copy-start | bytes 1368580
  100.9 1.1 copy-start.21
  101.0 1.1 copy-start.22
  101.0 1.1 copy-start.35
  101.0 14.1 %slice-start.2 = ((s8[4718592]{0:T(1024)(128)(4,1)}), s8[4194304]{0:T(1024)(128)(4,1)S(1)}, s32[]{:S(2)}) async-start(s8[4718592]{0:T(1024)(128)(4,1)} %bitcast.146), calls=%async_computation.13 | async-start | bytes 8388608
  101.0 18.4 %slice-start = ((s8[4718592]{0:T(1024)(128)(4,1)}), s8[4194304]{0:T(1024)(128)(4,1)S(1)}, s32[]{:S(2)}) async-start(s8[4718592]{0:T(1024)(128)(4,1)} %bitcast.144), calls=%async_computation.11 | async-start | bytes 8388608
  101.7 20.8 %copy-start.3 = (f32[1,297,768]{2,1,0:T(8,128)}, f32[1,297,768]{2,1,0:T(8,128)S(1)}, u32[]{:S(2)}) copy-start(f32[1,297,768]{2,1,0:T(8,128)S(1)} %get-tuple-element.46) | copy-start | bytes 2737156
  102.0 20.4 %copy-start.25 = (f32[297]{0:T(512)}, f32[297]{0:T(512)S(1)}, u32[]{:S(2)}) copy-start(f32[297]{0:T(512)S(1)} %add_rsqrt_fusion) | copy-start | bytes 3568
  102.0 13.1 %copy-start.17 = (bf16[1,297,768]{2,1,0:T(8,128)(2,1)S(1)}, bf16[1,297,768]{2,1,0:T(8,128)(2,1)}, u32[]{:S(2)}) copy-start(bf16[1,297,768]{2,1,0:T(8,128)(2,1)} %param.18) | copy-start | bytes 1368580
  102.1 13.1 %slice-start.3 = ((s8[4718592]{0:T(1024)(128)(4,1)}), s8[524288]{0:T(1024)(128)(4,1)S(1)}, s32[]{:S(2)}) async-start(s8[4718592]{0:T(1024)(128)(4,1)} %bitcast.146), calls=%async_computation.14 | async-start | bytes 1048576
  102.1 17.4 %slice-start.1 = ((s8[4718592]{0:T(1024)(128)(4,1)}), s8[524288]{0:T(1024)(128)(4,1)S(1)}, s32[]{:S(2)}) async-start(s8[4718592]{0:T(1024)(128)(4,1)} %bitcast.144), calls=%async_computation.12 | async-start | bytes 1048576
  119.4 2.3 copy-start.16
  123.6 0.9 copy-start.2
  127.9 11.0 %copy-start.4 = (bf16[1,1188,768]{1,2,0:T(8,128)(2,1)S(1)}, bf16[1,1188,768]{1,2,0:T(8,128)(2,1)}, u32[]{:S(2)}) copy-start(bf16[1,1188,768]{1,2,0:T(8,128)(2,1)} %copy.45) | copy-start | bytes 5474308
  127.9 11.0 %copy-start.8 = (bf16[297,768]{0,1:T(8,128)(2,1)S(1)}, bf16[297,768]{0,1:T(8,128)(2,1)}, u32[]{:S(2)}) copy-start(bf16[297,768]{0,1:T(8,128)(2,1)} %copy.49) | copy-start | bytes 1368580
  127.9 11.0 %copy-start.20 = (f32[12,297]{1,0:T(8,128)S(1)}, f32[12,297]{1,0:T(8,128)}, u32[]{:S(2)}) copy-start(f32[12,297]{1,0:T(8,128)} %log_add_fusion) | copy-start | bytes 42772
  151.3 12.8 %copy-start.7 = (bf16[1,297,768]{1,2,0:T(8,128)(2,1)S(1)}, bf16[1,297,768]{1,2,0:T(8,128)(2,1)}, u32[]{:S(2)}) copy-start(bf16[1,297,768]{1,2,0:T(8,128)(2,1)} %copy.46) | copy-start | bytes 1368580
  164.2 4.3 copy-start.1
  168.5 3.7 copy-start.38
  168.5 186.6 %reduce-scatter.9.cloned.1.call-start = ((), (), s32[]{:S(2)}) async-start(), calls=%async_computation.7 | async-start | bytes 2433024 | tf_op jit(solution)/shard_map/reduce_scatter | solution.py:189
  172.1 308.1 %reduce-scatter.7.cloned.1.call-start = ((), (), s32[]{:S(2)}) async-start(), calls=%async_computation.6 | async-start | bytes 7299072 | tf_op jit(solution)/shard_map/reduce_scatter | solution.py:186
  173.4 81.3 %copy-start.23 = (f32[768]{0:T(1024)S(1)}, f32[768]{0:T(1024)}, u32[]{:S(2)}) copy-start(f32[768]{0:T(1024)} %param.21) | copy-start | bytes 9220
  252.3 1.6 copy-start.11
  253.9 0.8 copy-start.13
  261.1 360.1 %reduce-scatter.11.cloned.1.call-start = ((), (), s32[]{:S(2)}) async-start(), calls=%async_computation.8 | async-start | bytes 9732096 | tf_op jit(solution)/shard_map/reduce_scatter | solution.py:191
  269.7 0.7 copy-start.29
  269.7 493.7 %reduce-scatter.13.cloned.1.call-start = ((), (), s32[]{:S(2)}) async-start(), calls=%async_computation.9 | async-start | bytes 9732096 | tf_op jit(solution)/shard_map/reduce_scatter | solution.py:193
  278.3 0.7 copy-start.24
  279.7 5.8 copy-start.6
  279.7 5.8 copy-start.10
  279.7 5.8 copy-start.12
  279.7 5.8 copy-start.14
  279.7 5.8 copy-start.27
  279.7 5.8 copy-start.31
  285.6 4.2 copy-start.32
  288.1 0.9 copy-start.9
Sparse Core Ops, SparseCore 0:
  16.3 34.0 all-gather.4
  52.0 31.3 all-gather.2
  168.6 81.4 all-reduce.14
  255.8 99.2 reduce-scatter.8
  362.1 118.1 reduce-scatter.6
  486.6 134.6 reduce-scatter.10
  628.7 134.5 reduce-scatter.12
where the time goes:
time: 775 us; the launch traced here: 770 us
  waiting for transfers between devices  510 us (66%)
  matrix products  115 us (15%)
  local copies, waits for them, and re-layouts  47.1 us (6%)
  blocking collectives  41.3 us (5%)
  other arithmetic  39.5 us (5%)
  between operations  16.2 us (2%)
    reduce_scatter x1, waiting for transfers between devices, on_device(): lax.psum_scatter(g_down_weight, ('clip', 'freq'), scatter_dimension=0, ti...  142 us
    reduce_scatter x1, waiting for transfers between devices, on_device(): lax.psum_scatter(g_up_weight, ('clip', 'freq'), scatter_dimension=0, tile...  141 us
    reduce_scatter x1, waiting for transfers between devices, on_device(): lax.psum_scatter(g_qkv_weight, ('clip', 'freq'), scatter_dimension=0, til...  125 us
    unnamed x8, waiting for transfers between devices  67.9 us
    unnamed x1, blocking collectives  41.3 us
    dot_general x4, matrix products, outer_sum(): jnp.einsum('crd,cre->de', left, right, preferred_element_type=jnp.float32)  26.2 us
    all_gather x1, waiting for transfers between devices, on_device(): lax.all_gather(key_rows, 'freq', axis=1, tiled=True)  23.7 us
    unnamed x97, local copies, waits for them, and re-layouts  20.2 us
  transfers between devices with their start and end apart: 7, of which 7 were waited for; matrix products, arithmetic and copies ran while one was open for 14% of the time, Pallas kernels for 0%

commit v1 on v0

--- a/solution.py
+++ b/solution.py
@@ -1,19 +1,228 @@
+import functools
+
 import jax
 import jax.numpy as jnp
 from jax import lax
+from jax.experimental import pallas as pl
+from jax.experimental.pallas import tpu as pltpu
 from jax.sharding import PartitionSpec as P
 
 HEADS = 12
+HEAD_DIM = 64
 TIME_COLS = 99
-
-
 EPS = 1e-06
+F32 = jnp.float32
+BF16 = jnp.bfloat16
+MESH = pl.DeviceIdType.MESH
+NT = (((1,), (1,)), ((), ()))
+TN = (((0,), (0,)), ((), ()))
+WIN = 256
+GROUP = 4
+
+
+def nt_dot(left, right):
+    return lax.dot_general(left, right, NT, preferred_element_type=F32)
+
+
+def tn_dot(left, right):
+    return lax.dot_general(left, right, TN, preferred_element_type=F32)
+
+
+def dot(left, right):
+    return jnp.dot(left, right, preferred_element_type=F32)
+
+
+def flip(index, stride):
+    return index + stride - 2 * stride * ((index // stride) % 2)
+
+
+def window_start(freq):
+    return pl.multiple_of((freq // 2) * 384 + (freq % 2) * 128, 128)
 
 
 def layer_stats(values):
     center = values - jnp.mean(values, -1, keepdims=True)
     inv_std = lax.rsqrt(jnp.mean(center * center, -1, keepdims=True) + EPS)
-    return (center * inv_std, inv_std)
+    return center * inv_std, inv_std
+
+
+def head_lanes(core, head):
+    lane = lax.broadcasted_iota(jnp.int32, (1, WIN), 1)
+    first = 64 * core + 64 * head
+    return (lane >= first) & (lane < first + 64)
+
+
+def spare_lane(core, which):
+    lane = lax.broadcasted_iota(jnp.int32, (1, WIN), 1)
+    return lane == 192 * (1 - core) + which
+
+
+def live_rows(shape, freq, keep_ref, length_ref, rows):
+    slot = lax.broadcasted_iota(jnp.int32, shape, 0)
+    live = jnp.zeros(shape, F32)
+    per = rows // TIME_COLS
+    for row in range(per):
+        column = slot - row * TIME_COLS
+        inside = (column >= 0) & (column < TIME_COLS) & (column < length_ref[0])
+        kept = (keep_ref[0, freq * per + row] > 0).astype(F32)
+        live = jnp.where(inside, kept, live)
+    return live
+
+
+def freq_device(freq):
+    return (lax.axis_index("clip"), freq)
+
+
+def attend_kernel(
+    rows, pad, tok_ref, gain_ref, shift_ref, weight_hbm, qbias_ref, vbias_ref, keep_ref, length_ref,
+    attn_ref, exp_hbm, q_ref, k_ref, v_ref, out_ref, inv_ref, first_ref, tok_all,
+    weight, exp_buf, out_low, attn_in,
+    w_sem, e_sem, near_send, near_recv, far_send, far_recv, fwd_send, fwd_recv, out_send, out_recv,
+):
+    freq = lax.axis_index("freq")
+    core = freq % 2
+    start = window_start(freq)
+    near, far, cross = flip(freq, 1), flip(freq, 2), flip(flip(freq, 1), 2)
+    loads = []
+    for part in range(3):
+        load = pltpu.make_async_copy(
+            weight_hbm.at[:, pl.ds(pl.multiple_of(start + 768 * part, 128), WIN)], weight.at[part], w_sem.at[part]
+        )
+        load.start()
+        loads.append(load)
+    barrier = pltpu.get_barrier_semaphore()
+    for other in (near, far, cross):
+        pl.semaphore_signal(barrier, inc=1, device_id=freq_device(other), device_id_type=MESH)
+    tok_all[freq, pad - 16 : pad, :] = jnp.zeros((16, 768), BF16)
+    tok_all[freq, 0:rows, :] = tok_ref[0]
+    pl.semaphore_wait(barrier, 3)
+
+    cuts = [(0, 80), (80, 80), (160, 80), (240, pad - 240)]
+    far_copies = []
+    for part, (first, count) in enumerate(cuts):
+        copy = pltpu.make_async_remote_copy(
+            src_ref=tok_all.at[freq, pl.ds(first, count)],
+            dst_ref=tok_all.at[freq, pl.ds(first, count)],
+            send_sem=far_send.at[part], recv_sem=far_recv.at[part],
+            device_id=freq_device(far), device_id_type=MESH,
+        )
+        copy.start()
+        far_copies.append(copy)
+    near_copy = pltpu.make_async_remote_copy(
+        src_ref=tok_all.at[freq], dst_ref=tok_all.at[freq], send_sem=near_send, recv_sem=near_recv,
+        device_id=freq_device(near), device_id_type=MESH,
+    )
+    near_copy.start()
+
+    def project(slot):
+        base = pl.multiple_of(slot * pad, 16)
+        span = pl.ds(base, pad)
+        normed, _ = layer_stats(tok_all[slot].astype(F32))
+        low = (normed * gain_ref[...] + shift_ref[...]).astype(BF16)
+        first_ref[span, :] = low
+        live = live_rows((pad, 1), slot, keep_ref, length_ref, rows)
+        queries = (dot(low, weight[0]) + qbias_ref[:, pl.ds(start, WIN)]).astype(BF16).astype(F32) * 0.125
+        keys = dot(low, weight[1])
+        values = dot(low, weight[2]) + vbias_ref[:, pl.ds(start, WIN)]
+        one = spare_lane(core, 0)
+        both = one | spare_lane(core, 1)
+        q_ref[span, :] = jnp.where(one, 1.0, queries).astype(BF16)
+        k_ref[span, :] = jnp.where(one, (live - 1.0) * 1e30, keys).astype(BF16)
+        v_ref[span, :] = jnp.where(both, 1.0, values).astype(BF16)
+
+    for load in loads:
+        load.wait()
+    project(freq)
+    near_copy.wait()
+    project(near)
+    forwards = []
+    for part, (first, count) in enumerate(cuts):
+        far_copies[part].wait()
+        copy = pltpu.make_async_remote_copy(
+            src_ref=tok_all.at[far, pl.ds(first, count)],
+            dst_ref=tok_all.at[far, pl.ds(first, count)],
+            send_sem=fwd_send.at[part], recv_sem=fwd_recv.at[part],
+            device_id=freq_device(near), device_id_type=MESH,
+        )
+        copy.start()
+        forwards.append(copy)
+    project(far)
+    for copy in forwards:
+        copy.wait()
+    project(cross)
+
+    sends, saves = [], []
+    for turn, slot in enumerate((far, cross, near, freq)):
+        base = pl.multiple_of(slot * pad, 16)
+        span = pl.ds(base, pad)
+        q_rows = q_ref[span, :]
+        total = jnp.zeros((pad, WIN), F32)
+        inverse = jnp.zeros((pad, WIN), F32)
+        for head in range(3):
+            lanes = head_lanes(core, head)
+            q_head = jnp.where(lanes | spare_lane(core, 0), q_rows, jnp.zeros_like(q_rows))
+            scores = nt_dot(q_head, k_ref[...])
+            exps = jnp.exp(scores - jnp.max(scores, -1, keepdims=True)).astype(BF16)
+            exp_buf[head, span, :] = exps
+            mixed = dot(exps, v_ref[...])
+            denom = jnp.sum(jnp.where(spare_lane(core, 0), mixed, 0.0), -1, keepdims=True)
+            scale = 1.0 / denom
+            total = jnp.where(lanes, mixed * scale, total)
+            inverse = jnp.where(lanes, scale, inverse)
+        save = pltpu.make_async_copy(exp_buf.at[:, span], exp_hbm.at[:, span], e_sem.at[turn])
+        save.start()
+        saves.append(save)
+        out_ref[span, :] = total
+        inv_ref[span, :] = inverse
+        if turn == 3:
+            attn_in[freq] = total.astype(BF16)
+        else:
+            out_low[span, :] = total.astype(BF16)
+            copy = pltpu.make_async_remote_copy(
+                src_ref=out_low.at[span], dst_ref=attn_in.at[freq],
+                send_sem=out_send.at[turn], recv_sem=out_recv.at[turn],
+                device_id=freq_device(slot), device_id_type=MESH,
+            )
+            copy.start()
+            sends.append(copy)
+    for copy in sends:
+        copy.wait()
+    for half in range(2):
+        left, right = attn_in[2 * half], attn_in[2 * half + 1]
+        at = 384 * half
+        attn_ref[:, at : at + 128] = left[:, 0:128]
+        attn_ref[:, at + 128 : at + 256] = (left[:, 128:256].astype(F32) + right[:, 0:128].astype(F32)).astype(BF16)
+        attn_ref[:, at + 256 : at + 384] = right[:, 128:256]
+    for save in saves:
+        save.wait()
+
+
+def attend(tokens, gain, shift, weight, qbias, vbias, keep, lengths):
+    rows, width = tokens.shape[1:]
+    pad = -(-rows // 16) * 16
+    slots = GROUP * pad
+    vm = pl.BlockSpec(memory_space=pltpu.VMEM)
+    sm = pl.BlockSpec(memory_space=pltpu.SMEM)
+    hbm = pl.BlockSpec(memory_space=pl.ANY)
+    sd = jax.ShapeDtypeStruct
+    dma = pltpu.SemaphoreType.DMA
+    return pl.pallas_call(
+        functools.partial(attend_kernel, rows, pad),
+        out_shape=(
+            sd((pad, width), BF16), sd((3, slots, slots), BF16), sd((slots, WIN), BF16), sd((slots, WIN), BF16),
+            sd((slots, WIN), BF16), sd((slots, WIN), F32), sd((slots, WIN), F32), sd((slots, width), BF16),
+            sd((GROUP, pad, width), BF16),
+        ),
+        in_specs=[vm, vm, vm, hbm, vm, vm, sm, sm],
+        out_specs=[vm, hbm, vm, vm, vm, vm, vm, vm, vm],
+        scratch_shapes=[
+            pltpu.VMEM((3, width, WIN), BF16), pltpu.VMEM((3, slots, slots), BF16), pltpu.VMEM((slots, WIN), BF16),
+            pltpu.VMEM((GROUP, pad, WIN), BF16),
+            dma((3,)), dma((4,)), dma, dma, dma((4,)), dma((4,)), dma((4,)), dma((4,)), dma((3,)), dma((3,)),
+        ],
+        compiler_params=pltpu.CompilerParams(collective_id=0, has_side_effects=True, vmem_limit_bytes=56 << 20),
+        name="attend",
+    )(tokens, gain.reshape(1, -1), shift.reshape(1, -1), weight, qbias.reshape(1, -1), vbias.reshape(1, -1), keep, lengths)
 
 
 def norm_back(grad_norm, normed, inv_std, gain):
@@ -100,15 +309,10 @@
 
     scores = scores_of(key_all)
     row_max = jnp.max(scores, -1, keepdims=True)
-    exp_scores = jnp.exp(scores - row_max)
-    row_total = jnp.sum(exp_scores, -1, keepdims=True)
-    attn_prob = exp_scores / row_total
-    log_total = row_max + jnp.log(row_total)
-    prob_low = attn_prob.astype(jnp.bfloat16)
-    mixed_heads = jnp.einsum(
-        "chrs,cshd->crhd", prob_low, head_split(value_all), preferred_element_type=jnp.float32
-    )
-    attn_rows = mixed_heads.reshape(clip_count, row_count, model_width).astype(jnp.bfloat16)
+    log_total = row_max + jnp.log(jnp.sum(jnp.exp(scores - row_max), -1, keepdims=True))
+    attn_rows = attend(
+        tokens, first_gain, first_shift, qkv_weight, query_bias, value_bias, freq_keep, lengths
+    )[0][None, :row_count]
     mid_rows = inputs + (
         jnp.dot(attn_rows, proj_weight, preferred_element_type=jnp.float32) + proj_bias
     )

time: 775 us -> 707 us (0.912)
  waiting for transfers between devices: 510 us -> 416 us
  Pallas kernels: 0 us -> 44.4 us
  other arithmetic: 39.5 us -> 30.7 us
  matrix products: 115 us -> 107 us
    reduce_scatter x1, waiting for transfers between devices: 141 us -> 95.3 us  [on_device(): lax.psum_scatter(g_up_weight, ('clip', 'freq'), scatter_dimension=0, tile...]
    pallas_call x0 -> x1, Pallas kernels: none -> 44.4 us  [attend(): pl.pallas_call(functools.partial(attend_kernel, rows, pad), out_shape=(sd...]
    all_gather x1, waiting for transfers between devices: 23.7 us -> 0.02 us  [on_device(): lax.all_gather(key_rows, 'freq', axis=1, tiled=True)]
    unnamed x8, waiting for transfers between devices: 67.9 us -> 54.8 us
    dot_general x1 -> x0, matrix products: 8.9 us -> none  [on_device(): jnp.einsum('chrs,cshd->crhd', prob_low, head_split(value_all), preferred_...]
    reduce_scatter x1, waiting for transfers between devices: 8.53 us -> 0.01 us  [on_device(): lax.psum_scatter(g_proj_weight, ('clip', 'freq'), scatter_dimension=0, ti...]
    unnamed x97 -> x73, local copies, waits for them, and re-layouts: 20.2 us -> 21.4 us
  transfers between devices with their start and end apart: 7 -> 7, of which waited for: 7 -> 4; matrix products, arithmetic and copies ran while one was open for 14% -> 18% of each run, Pallas kernels for 0% -> 6%
where the time goes in v1:
time: 707 us; the launch traced here: 702 us
  waiting for transfers between devices  416 us (59%)
  matrix products  107 us (15%)
  local copies, waits for them, and re-layouts  44.7 us (6%)
  Pallas kernels  44.4 us (6%)
  blocking collectives  41 us (6%)
  other arithmetic  30.7 us (4%)
  between operations  17.6 us (2%)
    reduce_scatter x1, waiting for transfers between devices, on_device(): lax.psum_scatter(g_down_weight, ('clip', 'freq'), scatter_dimension=0, ti...  141 us
    reduce_scatter x1, waiting for transfers between devices, on_device(): lax.psum_scatter(g_qkv_weight, ('clip', 'freq'), scatter_dimension=0, til...  125 us
    reduce_scatter x1, waiting for transfers between devices, on_device(): lax.psum_scatter(g_up_weight, ('clip', 'freq'), scatter_dimension=0, tile...  95.3 us
    unnamed x8, waiting for transfers between devices  54.8 us
    pallas_call x1, Pallas kernels, attend(): pl.pallas_call(functools.partial(attend_kernel, rows, pad), out_shape=(sd...  44.4 us
    unnamed x1, blocking collectives  41 us
    dot_general x4, matrix products, outer_sum(): jnp.einsum('crd,cre->de', left, right, preferred_element_type=jnp.float32)  25.2 us
    unnamed x73, local copies, waits for them, and re-layouts  21.4 us
  transfers between devices with their start and end apart: 7, of which 4 were waited for; matrix products, arithmetic and copies ran while one was open for 18% of the time, Pallas kernels for 6%

profile of v1, /device:TPU:0, one launch (start us, length us, event | category | flops | bytes accessed | tf_op | source)
XLA Modules:
  0.0 702.3 jit_solution(3928516559820026703)
XLA Ops:
  8.1 1.3 convert_reduce_fusion.1
  9.3 1.3 fusion.35
  10.7 3.6 convolution_bitcast_fusion
  14.3 1.6 copy-done.16
  15.9 1.6 copy.43
  17.6 1.6 fusion.36
  19.3 1.6 copy.47
  20.9 0.5 all-reduce.15.cloned.1.call-start
  22.6 0.6 reshape.475.qbias_ref
  23.2 0.6 reshape.476.vbias_ref
  23.8 0.6 reshape.474.shift_ref
  24.4 0.6 reshape.473.gain_ref
  24.9 1.1 copy.45
  26.0 44.4 %attend.1 = (bf16[304,768]{1,0:T(8,128)(2,1)}, bf16[3,1216,1216]{2,1,0:T(8,128)(2,1)}, bf16[1216,256]{1,0:T(8,128)(2,1)}, bf16[1216,256]{1,0:T(8,128)(2,1)}, bf1...) custom-call(bf16[1,297,768]{2,1,0:T(8,128)(2,1)} %tok_ref.1, ...), custom_call_target="tpu_custom_call" | custom-call | tf_op jit(solution)/shard_map/attend/pallas_call | solution.py:209
  70.5 1.9 fusion.75
  72.4 0.3 multiply_reduce_fusion.1
  72.8 12.7 %multiply_convert_fusion.1 = (bf16[297,3072]{1,0:T(8,128)(2,1)}, f32[297,3072]{1,0:T(8,128)S(1)}, f32[297,3072]{1,0:T(8,128)S(1)}) fusion(f32[3072]{0:T(1024)S(1)} %copy-done.27, bf16[768,3072]{1,0:T(8,128)(2,1)} %param.30, f32[1,297,768]{2,1,0:T(8,128)S(1)} %get-tuple-element.46, f32[768]{0:T(1024)S(1)} %copy-done.21, f32[768]{0:T(1024)S(1)} %copy-done.20, ...), kind=kOutput, calls=%fused_computation.16 | convolution fusion | flops 1462779648 | bytes 14775624 | tf_op jit(solution)/shard_map/dot_general | solution.py:321
  85.5 6.8 convert_reduce_fusion
  92.3 5.5 fusion.38
  98.0 0.5 convert_reduce_fusion.5
  98.5 0.9 copy-done.3
  99.4 0.6 convolution_convert_fusion
  100.0 0.3 copy.46
  100.4 7.2 %copy.44 = bf16[1,1188,768]{1,2,0:T(8,128)(2,1)S(1)} copy(bf16[1,1188,768]{2,0,1:T(2,128)(2,1)} %all-gather.3.cloned.1.call-done) | data formatting | bytes 3649536 | tf_op jit(solution)/shard_map/all_gather | solution.py:289
  107.6 8.1 %fusion.76 = (f32[12,297]{1,0:T(8,128)S(1)}, f32[12,297,1188]{2,1,0:T(8,128)}) fusion(bf16[297,12,64]{0,2,1:T(8,128)(2,1)S(1)} %bitcast.127, bf16[1188,12,64]{0,2,1:T(8,128)(2,1)S(1)} %bitcast.122, pred[1188]{0:T(1024)(128)(4,1)S(1)} %and.44), kind=kOutput, calls=%fused_computation.121 | convolution fusion | flops 554654656 | bytes 19232532 | tf_op jit(solution)/shard_map/crhd,cshd->chrs/dot_general | solution.py:300
  115.7 9.1 %exponential_reduce_fusion = f32[12,297]{1,0:T(8,128)S(1)} fusion(f32[12,297,1188]{2,1,0:T(8,128)} %get-tuple-element.50, f32[12,297]{1,0:T(8,128)S(1)} %get-tuple-element.49), kind=kLoop, calls=%fused_computation.5 | loop fusion | flops 8464500 | bytes 16964640 | tf_op jit(solution)/shard_map/reduce_sum | solution.py:312
  124.8 9.0 %fusion.12 = bf16[12,64,1188]{2,1,0:T(8,128)(2,1)} fusion(bf16[297,12,64]{0,2,1:T(8,128)(2,1)S(1)} %bitcast.129, f32[12,297,1188]{2,1,0:T(8,128)} %get-tuple-element.50, f32[12,297]{1,0:T(8,128)S(1)} %log_add_fusion), kind=kOutput, calls=%fused_computation.31 | convolution fusion | flops 551336576 | bytes 19231344 | tf_op jit(solution)/shard_map/chrs,crhd->cshd/dot_general | solution.py:362
  133.8 8.6 %copy.48 = bf16[1,1188,768]{1,2,0:T(8,128)(2,1)} copy(bf16[1,1188,768]{2,0,1:T(2,128)(2,1)} %all-gather.5.cloned.1.call-done) | data formatting | bytes 3649536 | tf_op jit(solution)/shard_map/all_gather | solution.py:290
  142.4 12.6 %multiply_reduce_fusion = (f32[12,297]{1,0:T(8,128)S(1)}, f32[12,297,1188]{2,1,0:T(8,128)}) fusion(f32[12,297,1188]{2,1,0:T(8,128)} %get-tuple-element.50, f32[12,297]{1,0:T(8,128)S(1)} %log_add_fusion, bf16[297,12,64]{0,2,1:T(8,128)(2,1)S(1)} %bitcast.130, bf16[1188,12,64]{0,2,1:T(8,128)(2,1)} %bitcast.126), kind=kOutput, calls=%fused_computation.3 | convolution fusion | flops 554654656 | bytes 36181728 | tf_op jit(solution)/shard_map/crhd,cshd->chrs/dot_general | solution.py:345
  155.0 12.8 %multiply_convert_fusion = bf16[12,297,1188]{2,1,0:T(8,128)(2,1)S(1)} fusion(f32[12,297,1188]{2,1,0:T(8,128)} %get-tuple-element.52, f32[12,297,1188]{2,1,0:T(8,128)} %get-tuple-element.50, f32[12,297]{1,0:T(8,128)S(1)} %get-tuple-element.51, f32[12,297]{1,0:T(8,128)S(1)} %log_add_fusion), kind=kLoop, calls=%fused_computation.2 | loop fusion | flops 16936128 | bytes 42368832 | tf_op jit(solution)/shard_map/convert_element_type | solution.py:348
  167.8 4.1 fusion.11
  172.2 1.1 copy-done.4
  173.3 3.3 fusion.47
  176.7 8.8 %fusion.68 = f32[768,3072]{1,0:T(8,128)} fusion(bf16[297,3072]{1,0:T(8,128)(2,1)} %copy-done.17, f32[1,297,768]{2,1,0:T(8,128)} %copy-done.9, f32[768]{0:T(1024)S(1)} %copy-done.21, f32[768]{0:T(1024)S(1)} %copy-done.20, f32[297]{0:T(512)S(1)} %add_rsqrt_fusion.1, f32[297]{0:T(512)S(1)} %broadcast_multiply_fusion.5), kind=kOutput, calls=%fused_computation.117 | convolution fusion | flops 1402562304 | bytes 12182856 | tf_op jit(solution)/shard_map/crd,cre->de/dot_general | solution.py:238
  185.6 0.3 reduce-scatter.13.cloned.1.call-start
  185.9 0.7 copy-done.19
  186.6 7.9 %fusion.50 = f32[3072,768]{1,0:T(8,128)} fusion(bf16[297,3072]{1,0:T(8,128)(2,1)} %get-tuple-element.40, bf16[1,297,768]{2,1,0:T(8,128)(2,1)S(1)} %copy-done.19, f32[297]{0:T(512)S(1)} %fusion.59), kind=kOutput, calls=%fused_computation.91 | convolution fusion | flops 1402106112 | bytes 11719332 | tf_op jit(solution)/shard_map/crd,cre->de/dot_general | solution.py:238
  194.6 0.6 copy-done.30
  195.1 0.6 dynamic-slice
  196.4 6.8 convert_reduce_fusion.3
  203.2 54.7 %all-reduce.15.cloned.1.call-done = (bf16[1,1188,768]{1,2,0:T(8,128)(2,1)}, bf16[1,1188,768]{1,2,0:T(8,128)(2,1)}) async-done(((bf16[1,1188,768]{1,2,0:T(8,128)(2,1)}, bf16[1,1188,768]{1,2,0:T(8,128)(2,1)}), (bf16[1,1188,768]{1,2,0:T(8,128)(2,1)}, bf16[1,1188,768]{1,2,0:T(8,128)(2,1)})) %all-reduce.15.cloned.1.call-update) | async-done | bytes 3649552
  257.8 1.6 convert_reduce_fusion.2
  259.4 1.6 constant_dynamic-slice_fusion.1
  261.1 0.8 copy-done.15
  261.9 5.2 fusion.43
  267.1 1.2 copy-done.10
  268.2 0.6 copy-done.12
  268.9 4.8 fusion.20
  273.8 5.1 fusion.34
  279.1 41.0 %all-reduce.11 = (f32[768]{0:T(1024)}, f32[768]{0:T(1024)}, f32[768]{0:T(1024)}, f32[768]{0:T(1024)}, f32[768]{0:T(1024)}, /*index=5*/f32[768]{0:T(1024)}, f32[768]{0:T(1024)}, f32[3072]{0:T(1024)}, f32[768]{0:T(1024)}) all-reduce(f32[768]{0:T(1024)} %get-tuple-element.19, ...), channel_id=4, replica_groups=mesh['clip'=8,'freq'=4] {'clip','freq'}, use_global_device_ids=true, to_apply=%region_14.15.clone | all-reduce | flops 9216 | bytes 73728
  320.1 1.3 dynamic-slice.4
  321.3 1.3 dynamic-slice.5
  322.6 1.3 dynamic-slice.6
  323.9 1.3 dynamic-slice.7
  325.1 1.3 dynamic-slice.8
  326.4 1.3 dynamic-slice.9
  327.6 1.3 dynamic-slice.10
  328.9 1.3 dynamic-slice.12
  330.2 1.3 dynamic-slice.11
  331.4 0.7 broadcast_multiply_fusion
  332.1 1.1 fusion.33
  333.3 95.3 %reduce-scatter.11.cloned.1.call-done = f32[24,3072]{1,0:T(8,128)} async-done(((f32[768,3072]{1,0:T(8,128)}), f32[24,3072]{1,0:T(8,128)}) %reduce-scatter.11.cloned.1.call-update) | async-done | bytes 294928 | tf_op jit(solution)/shard_map/reduce_scatter | solution.py:395
  428.6 140.9 %reduce-scatter.13.cloned.1.call-done = f32[96,768]{1,0:T(8,128)} async-done(((f32[3072,768]{1,0:T(8,128)}), f32[96,768]{1,0:T(8,128)}) %reduce-scatter.13.cloned.1.call-update) | async-done | bytes 294928 | tf_op jit(solution)/shard_map/reduce_scatter | solution.py:397
  569.5 125.0 %reduce-scatter.7.cloned.1.call-done = f32[24,2304]{1,0:T(8,128)} async-done(((f32[768,2304]{1,0:T(8,128)}), f32[24,2304]{1,0:T(8,128)}) %reduce-scatter.7.cloned.1.call-update) | async-done | bytes 221200 | tf_op jit(solution)/shard_map/reduce_scatter | solution.py:390
  (90 shorter events, 1.8 us)
Async XLA Ops:
  8.0 62.5 %copy-start = (bf16[768,768]{1,0:T(8,128)(2,1)S(1)}, bf16[768,768]{1,0:T(8,128)(2,1)}, u32[]{:S(2)}) copy-start(bf16[768,768]{1,0:T(8,128)(2,1)} %param.26) | copy-start | bytes 3538948
  8.0 92.3 %all-gather.3.cloned.1.call-start = ((), (), s32[]{:S(2)}) async-start(), calls=%async_computation.4 | async-start | bytes 4561920 | tf_op jit(solution)/shard_map/all_gather | solution.py:289
  10.7 7.0 copy-start.23
  10.7 7.0 copy-start.24
  14.2 1.6 copy-start.16
  15.9 6.4 copy-start.26
  15.9 7.9 %copy-start.25 = (f32[768]{0:T(1024)S(1)}, f32[768]{0:T(1024)}, u32[]{:S(2)}) copy-start(f32[768]{0:T(1024)} %param.22) | copy-start | bytes 9220
  15.9 8.5 %copy-start.22 = (f32[768]{0:T(1024)S(1)}, f32[768]{0:T(1024)}, u32[]{:S(2)}) copy-start(f32[768]{0:T(1024)} %param.21) | copy-start | bytes 9220
  17.6 116.3 %all-gather.5.cloned.1.call-start = ((), (), s32[]{:S(2)}) async-start(), calls=%async_computation.5 | async-start | bytes 4561920 | tf_op jit(solution)/shard_map/all_gather | solution.py:290
  19.3 51.2 %copy-start.6 = (bf16[1,297,768]{2,1,0:T(8,128)(2,1)S(1)}, bf16[1,297,768]{2,1,0:T(8,128)(2,1)}, u32[]{:S(2)}) copy-start(bf16[1,297,768]{2,1,0:T(8,128)(2,1)} %tok_ref.1) | copy-start | bytes 1368580
  19.3 51.2 %copy-start.28 = (f32[768]{0:T(1024)S(1)}, f32[768]{0:T(1024)}, u32[]{:S(2)}) copy-start(f32[768]{0:T(1024)} %param.27) | copy-start | bytes 9220
  20.9 236.9 %all-reduce.15.cloned.1.call-start = ((), (), s32[]{:S(2)}) async-start(), calls=%async_computation.10 | async-start | bytes 7864320
  26.0 46.7 %copy-start.20 = (f32[768]{0:T(1024)S(1)}, f32[768]{0:T(1024)}, u32[]{:S(2)}) copy-start(f32[768]{0:T(1024)} %param.28) | copy-start | bytes 9220
  26.0 46.7 %copy-start.21 = (f32[768]{0:T(1024)S(1)}, f32[768]{0:T(1024)}, u32[]{:S(2)}) copy-start(f32[768]{0:T(1024)} %param.29) | copy-start | bytes 9220
  26.0 46.7 %copy-start.27 = (f32[3072]{0:T(1024)S(1)}, f32[3072]{0:T(1024)}, u32[]{:S(2)}) copy-start(f32[3072]{0:T(1024)} %param.31) | copy-start | bytes 36868
  72.4 25.6 %copy-start.9 = (f32[1,297,768]{2,1,0:T(8,128)}, f32[1,297,768]{2,1,0:T(8,128)S(1)}, u32[]{:S(2)}) copy-start(f32[1,297,768]{2,1,0:T(8,128)S(1)} %get-tuple-element.46) | copy-start | bytes 2737156
  72.8 12.7 %copy-start.18 = (bf16[1,297,768]{2,1,0:T(8,128)(2,1)S(1)}, bf16[1,297,768]{2,1,0:T(8,128)(2,1)}, u32[]{:S(2)}) copy-start(bf16[1,297,768]{2,1,0:T(8,128)(2,1)} %param.18) | copy-start | bytes 1368580
  92.3 5.5 copy-start.17
  98.5 1.0 copy-start.3
  100.0 7.6 %copy-start.11 = (bf16[1,297,768]{1,2,0:T(8,128)(2,1)S(1)}, bf16[1,297,768]{1,2,0:T(8,128)(2,1)}, u32[]{:S(2)}) copy-start(bf16[1,297,768]{1,2,0:T(8,128)(2,1)} %copy.45) | copy-start | bytes 1368580
  167.8 4.3 copy-start.2
  172.1 1.2 copy-start.4
  172.1 161.1 %reduce-scatter.9.cloned.1.call-start = ((), (), s32[]{:S(2)}) async-start(), calls=%async_computation.7 | async-start | bytes 2433024 | tf_op jit(solution)/shard_map/reduce_scatter | solution.py:393
  176.6 252.0 %reduce-scatter.11.cloned.1.call-start = ((), (), s32[]{:S(2)}) async-start(), calls=%async_computation.8 | async-start | bytes 9732096 | tf_op jit(solution)/shard_map/reduce_scatter | solution.py:395
  185.5 1.0 copy-start.19
  185.6 383.9 %reduce-scatter.13.cloned.1.call-start = ((), (), s32[]{:S(2)}) async-start(), calls=%async_computation.9 | async-start | bytes 9732096 | tf_op jit(solution)/shard_map/reduce_scatter | solution.py:397
  194.5 0.7 copy-start.30
  194.5 500.0 %reduce-scatter.7.cloned.1.call-start = ((), (), s32[]{:S(2)}) async-start(), calls=%async_computation.6 | async-start | bytes 7299072 | tf_op jit(solution)/shard_map/reduce_scatter | solution.py:390
  196.4 65.5 %copy-start.7 = (bf16[1,297,768]{2,1,0:T(8,128)(2,1)S(1)}, bf16[1,297,768]{2,1,0:T(8,128)(2,1)}, u32[]{:S(2)}) copy-start(bf16[1,297,768]{2,1,0:T(8,128)(2,1)} %tok_ref.1) | copy-start | bytes 1368580
  203.2 57.9 %copy-start.13 = (bf16[12,64,297]{2,1,0:T(8,128)(2,1)}, bf16[12,64,297]{2,1,0:T(8,128)(2,1)S(1)}, u32[]{:S(2)}) copy-start(bf16[12,64,297]{2,1,0:T(8,128)(2,1)S(1)} %get-tuple-element.55) | copy-start | bytes 1368580
  259.4 1.7 copy-start.14
  261.0 0.9 copy-start.15
  267.1 1.2 copy-start.10
  267.1 1.8 copy-start.12
  267.1 1.8 copy-start.29
  268.9 4.9 copy-start.8
  273.8 58.3 %copy-start.5 = (f32[1,297,768]{2,1,0:T(8,128)S(1)}, f32[1,297,768]{2,1,0:T(8,128)}, u32[]{:S(2)}) copy-start(f32[1,297,768]{2,1,0:T(8,128)} %copy-done.3) | copy-start | bytes 2737156
  273.8 420.7 %copy-start.1 = (bf16[768,768]{1,0:T(8,128)(2,1)S(1)}, bf16[768,768]{1,0:T(8,128)(2,1)}, u32[]{:S(2)}) copy-start(bf16[768,768]{1,0:T(8,128)(2,1)} %param.26) | copy-start | bytes 3538948
Sparse Core Ops, SparseCore 0:
  17.7 45.8 all-gather.2
  65.2 31.2 all-gather.4
  172.2 85.5 all-reduce.14
Sparse Core Ops, SparseCore 1:
  178.4 108.0 reduce-scatter.8
  293.9 134.7 reduce-scatter.10
  435.0 134.5 reduce-scatter.12
  576.7 117.7 reduce-scatter.6
